TPU v7x, 256 devices: a whole 4x4x8 slice. The times are simulated.
256 devices in a mesh: dp: 128 (over y_lo, z, x, core), section: 2 (over y_hi).
Axes of the slice: x: 4, y: 4 (y_hi: 2, y_lo: 2; y = y_hi * 2 + y_lo), z: 8, core: 2. Of those that a mesh axis runs over, the one named last changes fastest.
Arguments:
- teacher_image: bfloat16 [65536, 1536], P(('dp', 'section')), may hold values from -6 to 6
- teacher_proj: bfloat16 [1536, 1536], replicated, may hold values from -0.15625 to 0.15625
- teacher_text: bfloat16 [65536, 1536], P(('dp', 'section')), may hold values from -6 to 6
- image_feats: bfloat16 [65536, 768], P(('dp', 'section')), may hold values from -6 to 6
- text_feats: bfloat16 [65536, 768], P(('dp', 'section')), may hold values from -6 to 6
- image_proj: bfloat16 [768, 768], replicated, may hold values from -0.21875 to 0.21875
- text_proj: bfloat16 [768, 768], replicated, may hold values from -0.21875 to 0.21875
- class_ids: int32 [65536], P(('dp', 'section')), may hold values from 0 to 255
Outputs:
- grad_image_proj: float32 [768, 768], replicated
- grad_text_proj: float32 [768, 768], replicated
All inputs are finite; a program needn't handle non-finite values.
Results may differ from a plain program's by a relative error of at most 0.005.
Values may be sent and summed in bfloat16 or wider, within the bound.
No kernel may reach another device: no remote copies, remote signals or barrier semaphores. Data moves between devices by JAX's collectives and lax.ppermute only.
A program may use at most 128 MiB of HBM per device.

v0:
```python
import jax
import jax.numpy as jnp
from jax import lax
from jax.sharding import PartitionSpec as P

WINDOW = 4
epsilon = 1e-06
teacher_scale = 20.0
teacher_shift = -1.0
student_scale = 20.0
student_shift = -1.0


def passed_along(block, axis, distance):
    devices = range(lax.axis_size(axis))
    route = [((i - distance) % len(devices), i) for i in devices]
    return lax.ppermute(block, axis, route)


def unit_rows(raw_rows):
    row_len = jnp.sqrt(jnp.sum(raw_rows * raw_rows, axis=1, keepdims=True) + epsilon)
    return (raw_rows / row_len, row_len)


def pair_tile(teach_rows, image_rows, row_ids, teach_cols, text_cols, col_ids):
    teacher_dot = lax.dot_general(
        teach_rows, teach_cols, (((1,), (1,)), ((), ())), preferred_element_type=jnp.float32
    )
    labels = (row_ids[:, None] == col_ids[None, :]).astype(jnp.float32)
    target = 0.5 * jax.nn.sigmoid(teacher_scale * teacher_dot + teacher_shift) + 0.5 * labels
    logits = (
        student_scale
        * lax.dot_general(
            image_rows, text_cols, (((1,), (1,)), ((), ())), preferred_element_type=jnp.float32
        )
        + student_shift
    )
    scaled = ((jax.nn.sigmoid(logits) - target) / text_cols.shape[0]).astype(jnp.bfloat16)
    row_part = student_scale * jnp.dot(scaled, text_cols, preferred_element_type=jnp.float32)
    col_part = student_scale * lax.dot_general(
        scaled, image_rows, (((0,), (0,)), ((), ())), preferred_element_type=jnp.float32
    )
    return (row_part, col_part)


def weight_grad(feats, unit, length, grad):
    direction = (grad - unit * jnp.sum(unit * grad, axis=1, keepdims=True)) / length
    high = direction.astype(jnp.bfloat16)
    low = (direction - high.astype(jnp.float32)).astype(jnp.bfloat16)
    dims = (((0,), (0,)), ((), ()))
    first = lax.dot_general(feats, high, dims, preferred_element_type=jnp.float32)
    second = lax.dot_general(feats, low, dims, preferred_element_type=jnp.float32)
    return first + second


def local(
    teacher_image,
    teacher_proj,
    teacher_text,
    image_feats,
    text_feats,
    image_proj,
    text_proj,
    class_ids,
):
    teacher_unit, teacher_len = unit_rows(
        jnp.dot(teacher_image, teacher_proj, preferred_element_type=jnp.float32)
    )
    teacher_img = teacher_unit.astype(jnp.bfloat16)
    written_unit, written_len = unit_rows(teacher_text.astype(jnp.float32))
    teacher_txt = written_unit.astype(jnp.bfloat16)
    own_ids = class_ids.astype(jnp.bfloat16)
    image_unit, image_len = unit_rows(
        jnp.dot(image_feats, image_proj, preferred_element_type=jnp.float32)
    )
    image_emb = image_unit.astype(jnp.bfloat16)
    teach_rows, image_rows, row_ids = (
        lax.all_gather(teacher_img, "section", axis=0, tiled=True),
        lax.all_gather(image_emb, "section", axis=0, tiled=True),
        lax.all_gather(own_ids, "section", axis=0, tiled=True),
    )
    grad_rows = jnp.zeros((image_rows.shape[0], image_rows.shape[1]), jnp.float32)
    text_unit, text_len = unit_rows(
        jnp.dot(text_feats, text_proj, preferred_element_type=jnp.float32)
    )
    text_emb = text_unit.astype(jnp.bfloat16)
    panels = (teacher_txt, text_emb, own_ids)
    carried = jnp.zeros(text_unit.shape, jnp.float32)
    for offset in range(WINDOW):
        if offset > 0:
            panels = passed_along((panels[0], panels[1], panels[2]), "dp", 1)
            carried = passed_along(carried, "dp", 1)
        row_part, col_part = pair_tile(
            teach_rows, image_rows, row_ids, panels[0], panels[1], panels[2]
        )
        grad_rows = grad_rows + row_part
        carried = carried + col_part
    grad_txt = passed_along(carried, "dp", 1 - WINDOW)
    text_part = weight_grad(text_feats, text_unit, text_len, grad_txt)
    own_grads = lax.psum_scatter(
        grad_rows.astype(jnp.bfloat16), "section", scatter_dimension=0, tiled=True
    ).astype(jnp.float32)
    image_part = weight_grad(image_feats, image_unit, image_len, own_grads)
    image_total, text_total = lax.psum((image_part, text_part), ("dp", "section"))
    return (image_total, text_total)


def solution(mesh):
    in_specs = (
        P(("dp", "section"), None),
        P(),
        P(("dp", "section"), None),
        P(("dp", "section"), None),
        P(("dp", "section"), None),
        P(),
        P(),
        P(("dp", "section")),
    )
    out_specs = (P(), P())
    return jax.shard_map(local, mesh=mesh, in_specs=in_specs, out_specs=out_specs, check_vma=False)
```

profile of v0, /device:TPU:2, one launch (start us, length us, event | category | flops | bytes accessed | tf_op | source)
XLA Modules:
  0.0 433.6 jit_solution(15911521493191360860)
XLA Ops:
  7.2 4.1 multiply_reduce_fusion
  14.1 1.6 collective-permute-start.1
  17.2 12.8 %collective-permute-done = bf16[256,768]{1,0:T(8,128)(2,1)} collective-permute-done((bf16[256,768]{1,0:T(8,128)(2,1)S(1)}, bf16[256,768]{1,0:T(8,128)(2,1)}, u32[]{:S(2)}, u32[]{:S(2)}) %collective-permute-start) | collective-permute-done | bytes 393248 | tf_op jit(solution)/shard_map/ppermute | solution.py:17
  30.1 22.3 %all_gather.9 = bf16[512,768]{1,0:T(8,128)(2,1)S(1)} all-gather(bf16[256,768]{1,0:T(8,128)(2,1)S(1)} %fusion.74), channel_id=1, replica_groups=mesh['dp'=128,'section'=2] {'section'}, dimensions={0}, use_global_device_ids=true | all-gather | bytes 1179648 | tf_op jit(solution)/shard_map/all_gather | solution.py:79
  54.5 5.7 %all-gather = bf16[2,1,256]{2,1,0:T(2,128)(2,1)S(1)} all-gather(bf16[1,1,256]{2,1,0:T(2,128)(2,1)S(1)} %reshape.35), channel_id=1, replica_groups=mesh['dp'=128,'section'=2] {'section'}, dimensions={0}, use_global_device_ids=true | all-gather | bytes 1536 | tf_op jit(solution)/shard_map/all_gather | solution.py:80
  61.8 2.4 fusion.62
  64.7 3.1 collective-permute-start.9
  68.2 1.8 fusion.43
  70.0 4.9 %collective-permute-done.4 = bf16[256,1536]{1,0:T(8,128)(2,1)} collective-permute-done((bf16[256,1536]{1,0:T(8,128)(2,1)}, bf16[256,1536]{1,0:T(8,128)(2,1)}, u32[]{:S(2)}, u32[]{:S(2)}) %collective-permute-start.4) | collective-permute-done | bytes 786464 | tf_op jit(solution)/shard_map/ppermute | solution.py:17
  74.9 1.8 fusion.36
  77.0 1.4 fusion.60
  78.5 1.5 fusion.77
  79.9 1.4 fusion.59
  81.4 1.4 fusion.76
  82.7 4.7 %collective-permute-done.9 = f32[256,768]{1,0:T(8,128)S(1)} collective-permute-done((f32[256,768]{1,0:T(8,128)S(1)}, f32[256,768]{1,0:T(8,128)S(1)}, u32[]{:S(2)}, u32[]{:S(2)}) %collective-permute-start.9) | collective-permute-done | bytes 786464 | tf_op jit(solution)/shard_map/ppermute | solution.py:17
  87.5 1.3 fusion.2
  88.8 7.1 %collective-permute-done.7 = bf16[256,1536]{1,0:T(8,128)(2,1)S(1)} collective-permute-done((bf16[256,1536]{1,0:T(8,128)(2,1)}, bf16[256,1536]{1,0:T(8,128)(2,1)S(1)}, u32[]{:S(2)}, u32[]{:S(2)}) %collective-permute-start.7) | collective-permute-done | bytes 786464 | tf_op jit(solution)/shard_map/ppermute | solution.py:17
  96.6 1.4 fusion.61
  98.7 2.3 multiply_convert_fusion
  101.1 1.3 convolution_multiply_fusion.1
  102.5 2.0 collective-permute-done.10
  104.4 1.2 add.158
  106.1 11.0 %collective-permute-done.11 = f32[256,768]{1,0:T(8,128)S(1)} collective-permute-done((f32[256,768]{1,0:T(8,128)S(1)}, f32[256,768]{1,0:T(8,128)S(1)}, u32[]{:S(2)}, u32[]{:S(2)}) %collective-permute-start.11) | collective-permute-done | bytes 786464 | tf_op jit(solution)/shard_map/ppermute | solution.py:17
  118.1 18.6 %collective-permute-start.12 = (f32[256,768]{1,0:T(8,128)}, f32[256,768]{1,0:T(8,128)S(1)}, u32[]{:S(2)}, u32[]{:S(2)}) collective-permute-start(f32[256,768]{1,0:T(8,128)} %add.159), channel_id=1, source_target_pairs={{6,0},{8,2},{10,4},{12,6},{14,8},{16,10},{18,12},{20,14},{22,16},{... | collective-permute-start | bytes 2359304 | tf_op jit(solution)/shard_map/ppermute | solution.py:17
  136.7 1.3 fusion.63
  138.0 1.8 fusion.69
  139.8 2.1 add_bitcast_fusion.1
  142.0 5.8 %collective-permute-done.12 = f32[256,768]{1,0:T(8,128)S(1)} collective-permute-done((f32[256,768]{1,0:T(8,128)}, f32[256,768]{1,0:T(8,128)S(1)}, u32[]{:S(2)}, u32[]{:S(2)}) %collective-permute-start.12) | collective-permute-done | bytes 786464 | tf_op jit(solution)/shard_map/ppermute | solution.py:17
  148.7 2.1 add_bitcast_fusion
  150.8 271.2 %all-reduce.3.cloned.1.call-done = (f32[768,768]{0,1:T(8,128)}, f32[768,768]{0,1:T(8,128)}) async-done(((f32[768,768]{0,1:T(8,128)}, f32[768,768]{0,1:T(8,128)}), (f32[768,768]{0,1:T(8,128)}, f32[768,768]{0,1:T(8,128)})) %all-reduce.3.cloned.1.call-update) | async-done | bytes 4718608 | tf_op jit(solution)/shard_map/psum | solution.py:104
  422.0 3.2 copy.14
  425.1 1.9 copy.15
  (81 shorter events, 12.7 us)
Async XLA Ops:
  7.2 8.5 %copy-start = (bf16[768,768]{1,0:T(8,128)(2,1)S(1)}, bf16[768,768]{1,0:T(8,128)(2,1)}, u32[]{:S(2)}) copy-start(bf16[768,768]{1,0:T(8,128)(2,1)} %param.14) | copy-start | bytes 3538948
  7.2 54.7 %all-gather.3.cloned.1.call-start = ((), (), s32[]{:S(2)}) async-start(), calls=%async_computation.1 | async-start | bytes 2359296 | tf_op jit(solution)/shard_map/all_gather | solution.py:78
  11.4 1.2 copy-start.15
  11.4 1.3 copy-start.1
  12.5 3.2 copy-start.12
  12.5 124.2 %reduce-scatter.2.cloned.1.call-start = ((), (), s32[]{:S(2)}) async-start(), calls=%async_computation.2 | async-start | bytes 1179648 | tf_op jit(solution)/shard_map/reduce_scatter | solution.py:100
  12.6 41.9 %copy-start.16 = (bf16[256]{0:T(256)(128)(2,1)}, bf16[256]{0:T(256)(128)(2,1)S(1)}, u32[]{:S(2)}) copy-start(bf16[256]{0:T(256)(128)(2,1)S(1)} %convert_element_type.63) | copy-start | bytes 1540
  12.6 41.1 %collective-permute-start.2 = (bf16[256]{0:T(256)(128)(2,1)S(1)}, bf16[256]{0:T(256)(128)(2,1)}, u32[]{:S(2)}, u32[]{:S(2)}) collective-permute-start(bf16[256]{0:T(256)(128)(2,1)S(1)} %convert_element_type.63), channel_id=1, source_target_pairs={{254,0},{0,2},{2,4},{4,6},{6,8},{8,10},{10,12},{12,14},{14,16},{16... | collective-permute-start | bytes 1544 | tf_op jit(solution)/shard_map/ppermute | solution.py:17
  14.1 2.4 copy-start.5
  14.1 2.4 copy-start.10
  14.1 46.8 %collective-permute-start.1 = (bf16[256,1536]{1,0:T(8,128)(2,1)}, bf16[256,1536]{1,0:T(8,128)(2,1)}, u32[]{:S(2)}, u32[]{:S(2)}) collective-permute-start(bf16[256,1536]{1,0:T(8,128)(2,1)} %fusion.1), channel_id=1, source_target_pairs={{254,0},{0,2},{2,4},{4,6},{6,8},{8,10},{10,12},{12,14},{14,16},{16... | collective-permute-start | bytes 2359304 | tf_op jit(solution)/shard_map/ppermute | solution.py:17
  16.4 36.0 %copy-start.3 = (bf16[256,768]{1,0:T(8,128)(2,1)}, bf16[256,768]{1,0:T(8,128)(2,1)S(1)}, u32[]{:S(2)}) copy-start(bf16[256,768]{1,0:T(8,128)(2,1)S(1)} %fusion.73) | copy-start | bytes 1179652
  16.4 13.6 %collective-permute-start = (bf16[256,768]{1,0:T(8,128)(2,1)S(1)}, bf16[256,768]{1,0:T(8,128)(2,1)}, u32[]{:S(2)}, u32[]{:S(2)}) collective-permute-start(bf16[256,768]{1,0:T(8,128)(2,1)S(1)} %fusion.73), channel_id=1, source_target_pairs={{254,0},{0,2},{2,4},{4,6},{6,8},{8,10},{10,12},{12,14},{14,16},{16... | collective-permute-start | bytes 1179656 | tf_op jit(solution)/shard_map/ppermute | solution.py:17
  30.1 31.7 %collective-permute-start.3 = (bf16[256,768]{1,0:T(8,128)(2,1)}, bf16[256,768]{1,0:T(8,128)(2,1)}, u32[]{:S(2)}, u32[]{:S(2)}) collective-permute-start(bf16[256,768]{1,0:T(8,128)(2,1)} %collective-permute-done), channel_id=1, source_target_pairs={{254,0},{0,2},{2,4},{4,6},{6,8},{8,10},{10,12},{12,14},{14,16},{16... | collective-permute-start | bytes 1179656 | tf_op jit(solution)/shard_map/ppermute | solution.py:17
  53.6 7.2 %collective-permute-start.5 = (bf16[256]{0:T(256)(128)(2,1)}, bf16[256]{0:T(256)(128)(2,1)}, u32[]{:S(2)}, u32[]{:S(2)}) collective-permute-start(bf16[256]{0:T(256)(128)(2,1)} %collective-permute-done.2), channel_id=1, source_target_pairs={{254,0},{0,2},{2,4},{4,6},{6,8},{8,10},{10,12},{12,14},{14,16},{16... | collective-permute-start | bytes 1544 | tf_op jit(solution)/shard_map/ppermute | solution.py:17
  60.9 27.9 %collective-permute-start.8 = (bf16[256]{0:T(256)(128)(2,1)}, bf16[256]{0:T(256)(128)(2,1)S(1)}, u32[]{:S(2)}, u32[]{:S(2)}) collective-permute-start(bf16[256]{0:T(256)(128)(2,1)} %collective-permute-done.5), channel_id=1, source_target_pairs={{254,0},{0,2},{2,4},{4,6},{6,8},{8,10},{10,12},{12,14},{14,16},{16... | collective-permute-start | bytes 1544 | tf_op jit(solution)/shard_map/ppermute | solution.py:17
  60.9 14.1 %collective-permute-start.4 = (bf16[256,1536]{1,0:T(8,128)(2,1)}, bf16[256,1536]{1,0:T(8,128)(2,1)}, u32[]{:S(2)}, u32[]{:S(2)}) collective-permute-start(bf16[256,1536]{1,0:T(8,128)(2,1)} %collective-permute-done.1), channel_id=1, source_target_pairs={{254,0},{0,2},{2,4},{4,6},{6,8},{8,10},{10,12},{12,14},{14,16},{16... | collective-permute-start | bytes 2359304 | tf_op jit(solution)/shard_map/ppermute | solution.py:17
  61.7 34.8 %collective-permute-start.6 = (bf16[256,768]{1,0:T(8,128)(2,1)}, bf16[256,768]{1,0:T(8,128)(2,1)}, u32[]{:S(2)}, u32[]{:S(2)}) collective-permute-start(bf16[256,768]{1,0:T(8,128)(2,1)} %collective-permute-done.3), channel_id=1, source_target_pairs={{254,0},{0,2},{2,4},{4,6},{6,8},{8,10},{10,12},{12,14},{14,16},{16... | collective-permute-start | bytes 1179656 | tf_op jit(solution)/shard_map/ppermute | solution.py:17
  64.3 3.5 copy-start.4
  64.7 3.5 copy-start.14
  64.7 22.8 %collective-permute-start.9 = (f32[256,768]{1,0:T(8,128)S(1)}, f32[256,768]{1,0:T(8,128)S(1)}, u32[]{:S(2)}, u32[]{:S(2)}) collective-permute-start(f32[256,768]{1,0:T(8,128)S(1)} %convolution_multiply_fusion.3), channel_id=1, source_target_pairs={{254,0},{0,2},{2,4},{4,6},{6,8},{8,10},{10,12},{12,14},{14,16},{16... | collective-permute-start | bytes 2359304 | tf_op jit(solution)/shard_map/ppermute | solution.py:17
  76.7 19.2 %collective-permute-start.7 = (bf16[256,1536]{1,0:T(8,128)(2,1)}, bf16[256,1536]{1,0:T(8,128)(2,1)S(1)}, u32[]{:S(2)}, u32[]{:S(2)}) collective-permute-start(bf16[256,1536]{1,0:T(8,128)(2,1)} %collective-permute-done.4), channel_id=1, source_target_pairs={{254,0},{0,2},{2,4},{4,6},{6,8},{8,10},{10,12},{12,14},{14,16},{16... | collective-permute-start | bytes 2359304 | tf_op jit(solution)/shard_map/ppermute | solution.py:17
  78.5 10.3 %copy-start.6 = (bf16[512,256]{1,0:T(8,128)(2,1)}, bf16[512,256]{1,0:T(8,128)(2,1)S(1)}, u32[]{:S(2)}) copy-start(bf16[512,256]{1,0:T(8,128)(2,1)S(1)} %fusion.60) | copy-start | bytes 786436
  88.7 15.7 %collective-permute-start.10 = (f32[256,768]{1,0:T(8,128)}, f32[256,768]{1,0:T(8,128)}, u32[]{:S(2)}, u32[]{:S(2)}) collective-permute-start(f32[256,768]{1,0:T(8,128)} %fusion.2), channel_id=1, source_target_pairs={{254,0},{0,2},{2,4},{4,6},{6,8},{8,10},{10,12},{12,14},{14,16},{16... | collective-permute-start | bytes 2359304 | tf_op jit(solution)/shard_map/ppermute | solution.py:17
  101.0 320.9 %all-reduce.3.cloned.1.call-start = ((), (), s32[]{:S(2)}) async-start(), calls=%async_computation.3 | async-start | bytes 9437184 | tf_op jit(solution)/shard_map/psum | solution.py:104
  102.4 3.3 copy-start.8
  105.7 11.5 %collective-permute-start.11 = (f32[256,768]{1,0:T(8,128)S(1)}, f32[256,768]{1,0:T(8,128)S(1)}, u32[]{:S(2)}, u32[]{:S(2)}) collective-permute-start(f32[256,768]{1,0:T(8,128)S(1)} %add.158), channel_id=1, source_target_pairs={{254,0},{0,2},{2,4},{4,6},{6,8},{8,10},{10,12},{12,14},{14,16},{16... | collective-permute-start | bytes 2359304 | tf_op jit(solution)/shard_map/ppermute | solution.py:17
  118.1 29.6 %collective-permute-start.12 = (f32[256,768]{1,0:T(8,128)}, f32[256,768]{1,0:T(8,128)S(1)}, u32[]{:S(2)}, u32[]{:S(2)}) collective-permute-start(f32[256,768]{1,0:T(8,128)} %add.159), channel_id=1, source_target_pairs={{6,0},{8,2},{10,4},{12,6},{14,8},{16,10},{18,12},{20,14},{22,16},{... | collective-permute-start | bytes 2359304 | tf_op jit(solution)/shard_map/ppermute | solution.py:17
  138.0 1.9 copy-start.9
  138.0 1.9 copy-start.11
  142.0 6.0 %copy-start.13 = (bf16[256,768]{1,0:T(8,128)(2,1)S(1)}, bf16[256,768]{1,0:T(8,128)(2,1)}, u32[]{:S(2)}) copy-start(bf16[256,768]{1,0:T(8,128)(2,1)} %param.12) | copy-start | bytes 1179652
  421.9 3.2 copy-start.2
  (1 other events, 0.7 us)
Sparse Core Ops, SparseCore 0:
  12.6 45.1 all-gather.2
  101.2 28.7 reduce-scatter.1
  150.9 271.0 all-reduce.2
where the time goes:
time: 434 us
  waiting for transfers between devices  320 us (74%)
  matrix products  33 us (8%)
  blocking collectives  28.1 us (6%)
  starting transfers between devices  25.8 us (6%)
  between operations  14.1 us (3%)
  other arithmetic  6.48 us (1%)
  local copies, waits for them, and re-layouts  5.91 us (1%)
    psum x1, waiting for transfers between devices, local(): lax.psum((image_part, text_part), ('dp', 'section'))  271 us
    ppermute x13, waiting for transfers between devices, passed_along(): return lax.ppermute(block, axis, route)  49 us
    ppermute x13, starting transfers between devices, passed_along(): return lax.ppermute(block, axis, route)  25.7 us
    all_gather x1, blocking collectives, local(): lax.all_gather(image_emb, 'section', axis=0, tiled=True)  22.3 us
  transfers between devices with their start and end apart: 16, of which 9 were waited for; matrix products, arithmetic and copies ran while one was open for 7% of the time, Pallas kernels for 0%

commit v1 on v0

--- a/solution.py
+++ b/solution.py
@@ -101,7 +101,10 @@
         grad_rows.astype(jnp.bfloat16), "section", scatter_dimension=0, tiled=True
     ).astype(jnp.float32)
     image_part = weight_grad(image_feats, image_unit, image_len, own_grads)
-    image_total, text_total = lax.psum((image_part, text_part), ("dp", "section"))
+    update_the_array = lambda inner_x, row_axis, bus_axis: lax.psum(
+        lax.psum(inner_x, row_axis), bus_axis
+    )
+    image_total, text_total = update_the_array((image_part, text_part), "section", "dp")
     return (image_total, text_total)
 
 

time: 434 us -> 1390 us (3.20)
  waiting for transfers between devices: 320 us -> 1270 us
    psum x1 -> x2, waiting for transfers between devices: 271 us -> 1220 us  [the longest x1 1080 us: local(): lax.psum(lax.psum(inner_x, row_axis), bus_axis)]
  transfers between devices with their start and end apart: 16 -> 17, of which waited for: 9 -> 10; matrix products, arithmetic and copies ran while one was open for 7% -> 2% of each run, Pallas kernels for 0% -> 0%
where the time goes in v1:
time: 1390 us; the launch traced here: 1380 us
  waiting for transfers between devices  1270 us (91%)
  matrix products  33 us (2%)
  blocking collectives  28.1 us (2%)
  starting transfers between devices  25.8 us (2%)
  between operations  14.1 us (1%)
    psum x1, waiting for transfers between devices, local(): lax.psum(lax.psum(inner_x, row_axis), bus_axis)  1080 us
    psum x1, waiting for transfers between devices, local(): lax.psum(inner_x, row_axis)  133 us
    ppermute x13, waiting for transfers between devices, passed_along(): return lax.ppermute(block, axis, route)  49 us
  transfers between devices with their start and end apart: 17, of which 10 were waited for; matrix products, arithmetic and copies ran while one was open for 2% of the time, Pallas kernels for 0%

profile of v1, /device:TPU:2, one launch (start us, length us, event | category | flops | bytes accessed | tf_op | source)
XLA Modules:
  0.0 1378.9 jit_solution(17376942863826828389)
XLA Ops:
  7.2 4.1 multiply_reduce_fusion
  14.1 1.6 collective-permute-start.1
  17.2 12.8 collective-permute-done
  30.1 22.3 %all_gather.9 = bf16[512,768]{1,0:T(8,128)(2,1)S(1)} all-gather(bf16[256,768]{1,0:T(8,128)(2,1)S(1)} %fusion.74), channel_id=1, replica_groups=mesh['dp'=128,'section'=2] {'section'}, dimensions={0}, use_global_device_ids=true | all-gather | bytes 1179648 | tf_op jit(solution)/shard_map/all_gather | solution.py:79
  54.5 5.7 all-gather
  61.8 2.4 fusion.62
  64.7 3.1 collective-permute-start.9
  68.2 1.8 fusion.43
  70.0 4.9 collective-permute-done.4
  74.9 1.8 fusion.36
  77.0 1.4 fusion.60
  78.5 1.5 fusion.77
  79.9 1.4 fusion.59
  81.4 1.4 fusion.76
  82.7 4.7 collective-permute-done.9
  87.5 1.3 fusion.2
  88.8 7.1 collective-permute-done.7
  96.6 1.4 fusion.61
  98.7 2.3 multiply_convert_fusion
  101.1 1.3 convolution_multiply_fusion.1
  102.5 2.0 collective-permute-done.10
  106.1 11.0 collective-permute-done.11
  118.1 18.9 %collective-permute-start.12 = (f32[256,768]{1,0:T(8,128)}, f32[256,768]{1,0:T(8,128)S(1)}, u32[]{:S(2)}, u32[]{:S(2)}) collective-permute-start(f32[256,768]{1,0:T(8,128)} %add.163), channel_id=1, source_target_pairs={{6,0},{8,2},{10,4},{12,6},{14,8},{16,10},{18,12},{20,14},{22,16},{... | collective-permute-start | bytes 2359304 | tf_op jit(solution)/shard_map/ppermute | solution.py:17
  137.0 1.3 fusion.63
  138.3 1.8 fusion.69
  140.2 2.1 add_bitcast_fusion.1
  142.3 5.5 collective-permute-done.12
  148.7 2.1 add_bitcast_fusion
  150.8 132.7 %all-reduce.7.cloned.1.call-done = (f32[768,768]{0,1:T(8,128)}, f32[768,768]{0,1:T(8,128)}) async-done(((f32[768,768]{0,1:T(8,128)}, f32[768,768]{0,1:T(8,128)}), (f32[768,768]{0,1:T(8,128)}, f32[768,768]{0,1:T(8,128)})) %all-reduce.7.cloned.1.call-update) | async-done | bytes 4718608 | tf_op jit(solution)/shard_map/psum | solution.py:105
  283.5 1083.7 %all-reduce.5.cloned.1.call-done = (f32[768,768]{0,1:T(8,128)}, f32[768,768]{0,1:T(8,128)}) async-done(((f32[768,768]{0,1:T(8,128)}, f32[768,768]{0,1:T(8,128)}), (f32[768,768]{0,1:T(8,128)}, f32[768,768]{0,1:T(8,128)})) %all-reduce.5.cloned.1.call-update) | async-done | bytes 4718608 | tf_op jit(solution)/shard_map/psum | solution.py:104
  1367.2 3.2 copy.14
  1370.4 1.9 copy.15
  (84 shorter events, 14.0 us)
Async XLA Ops:
  7.2 8.5 copy-start
  7.2 54.7 %all-gather.3.cloned.1.call-start = ((), (), s32[]{:S(2)}) async-start(), calls=%async_computation.1 | async-start | bytes 2359296 | tf_op jit(solution)/shard_map/all_gather | solution.py:78
  11.4 1.3 copy-start.1
  12.5 3.2 copy-start.12
  12.5 124.5 %reduce-scatter.2.cloned.1.call-start = ((), (), s32[]{:S(2)}) async-start(), calls=%async_computation.2 | async-start | bytes 1179648 | tf_op jit(solution)/shard_map/reduce_scatter | solution.py:100
  12.6 41.9 %copy-start.16 = (bf16[256]{0:T(256)(128)(2,1)}, bf16[256]{0:T(256)(128)(2,1)S(1)}, u32[]{:S(2)}) copy-start(bf16[256]{0:T(256)(128)(2,1)S(1)} %convert_element_type.63) | copy-start | bytes 1540
  12.6 41.1 %collective-permute-start.2 = (bf16[256]{0:T(256)(128)(2,1)S(1)}, bf16[256]{0:T(256)(128)(2,1)}, u32[]{:S(2)}, u32[]{:S(2)}) collective-permute-start(bf16[256]{0:T(256)(128)(2,1)S(1)} %convert_element_type.63), channel_id=1, source_target_pairs={{254,0},{0,2},{2,4},{4,6},{6,8},{8,10},{10,12},{12,14},{14,16},{16... | collective-permute-start | bytes 1544 | tf_op jit(solution)/shard_map/ppermute | solution.py:17
  14.1 2.4 copy-start.5
  14.1 2.4 copy-start.10
  14.1 47.1 %collective-permute-start.1 = (bf16[256,1536]{1,0:T(8,128)(2,1)}, bf16[256,1536]{1,0:T(8,128)(2,1)}, u32[]{:S(2)}, u32[]{:S(2)}) collective-permute-start(bf16[256,1536]{1,0:T(8,128)(2,1)} %fusion.1), channel_id=1, source_target_pairs={{254,0},{0,2},{2,4},{4,6},{6,8},{8,10},{10,12},{12,14},{14,16},{16... | collective-permute-start | bytes 2359304 | tf_op jit(solution)/shard_map/ppermute | solution.py:17
  16.4 36.0 %copy-start.3 = (bf16[256,768]{1,0:T(8,128)(2,1)}, bf16[256,768]{1,0:T(8,128)(2,1)S(1)}, u32[]{:S(2)}) copy-start(bf16[256,768]{1,0:T(8,128)(2,1)S(1)} %fusion.73) | copy-start | bytes 1179652
  16.4 13.6 collective-permute-start
  30.1 31.7 %collective-permute-start.3 = (bf16[256,768]{1,0:T(8,128)(2,1)}, bf16[256,768]{1,0:T(8,128)(2,1)}, u32[]{:S(2)}, u32[]{:S(2)}) collective-permute-start(bf16[256,768]{1,0:T(8,128)(2,1)} %collective-permute-done), channel_id=1, source_target_pairs={{254,0},{0,2},{2,4},{4,6},{6,8},{8,10},{10,12},{12,14},{14,16},{16... | collective-permute-start | bytes 1179656 | tf_op jit(solution)/shard_map/ppermute | solution.py:17
  53.6 7.5 collective-permute-start.5
  61.2 27.6 %collective-permute-start.8 = (bf16[256]{0:T(256)(128)(2,1)}, bf16[256]{0:T(256)(128)(2,1)S(1)}, u32[]{:S(2)}, u32[]{:S(2)}) collective-permute-start(bf16[256]{0:T(256)(128)(2,1)} %collective-permute-done.5), channel_id=1, source_target_pairs={{254,0},{0,2},{2,4},{4,6},{6,8},{8,10},{10,12},{12,14},{14,16},{16... | collective-permute-start | bytes 1544 | tf_op jit(solution)/shard_map/ppermute | solution.py:17
  61.2 13.8 collective-permute-start.4
  61.7 34.8 %collective-permute-start.6 = (bf16[256,768]{1,0:T(8,128)(2,1)}, bf16[256,768]{1,0:T(8,128)(2,1)}, u32[]{:S(2)}, u32[]{:S(2)}) collective-permute-start(bf16[256,768]{1,0:T(8,128)(2,1)} %collective-permute-done.3), channel_id=1, source_target_pairs={{254,0},{0,2},{2,4},{4,6},{6,8},{8,10},{10,12},{12,14},{14,16},{16... | collective-permute-start | bytes 1179656 | tf_op jit(solution)/shard_map/ppermute | solution.py:17
  64.3 3.5 copy-start.4
  64.7 3.5 copy-start.14
  64.7 22.8 %collective-permute-start.9 = (f32[256,768]{1,0:T(8,128)S(1)}, f32[256,768]{1,0:T(8,128)S(1)}, u32[]{:S(2)}, u32[]{:S(2)}) collective-permute-start(f32[256,768]{1,0:T(8,128)S(1)} %convolution_multiply_fusion.3), channel_id=1, source_target_pairs={{254,0},{0,2},{2,4},{4,6},{6,8},{8,10},{10,12},{12,14},{14,16},{16... | collective-permute-start | bytes 2359304 | tf_op jit(solution)/shard_map/ppermute | solution.py:17
  76.7 19.2 %collective-permute-start.7 = (bf16[256,1536]{1,0:T(8,128)(2,1)}, bf16[256,1536]{1,0:T(8,128)(2,1)S(1)}, u32[]{:S(2)}, u32[]{:S(2)}) collective-permute-start(bf16[256,1536]{1,0:T(8,128)(2,1)} %collective-permute-done.4), channel_id=1, source_target_pairs={{254,0},{0,2},{2,4},{4,6},{6,8},{8,10},{10,12},{12,14},{14,16},{16... | collective-permute-start | bytes 2359304 | tf_op jit(solution)/shard_map/ppermute | solution.py:17
  78.5 10.3 copy-start.6
  88.7 15.7 %collective-permute-start.10 = (f32[256,768]{1,0:T(8,128)}, f32[256,768]{1,0:T(8,128)}, u32[]{:S(2)}, u32[]{:S(2)}) collective-permute-start(f32[256,768]{1,0:T(8,128)} %fusion.2), channel_id=1, source_target_pairs={{254,0},{0,2},{2,4},{4,6},{6,8},{8,10},{10,12},{12,14},{14,16},{16... | collective-permute-start | bytes 2359304 | tf_op jit(solution)/shard_map/ppermute | solution.py:17
  101.1 182.5 %all-reduce.7.cloned.1.call-start = ((), (), s32[]{:S(2)}) async-start(), calls=%async_computation.4 | async-start | bytes 9437184 | tf_op jit(solution)/shard_map/psum | solution.py:105
  102.4 3.3 copy-start.8
  105.7 11.5 collective-permute-start.11
  118.1 29.6 %collective-permute-start.12 = (f32[256,768]{1,0:T(8,128)}, f32[256,768]{1,0:T(8,128)S(1)}, u32[]{:S(2)}, u32[]{:S(2)}) collective-permute-start(f32[256,768]{1,0:T(8,128)} %add.163), channel_id=1, source_target_pairs={{6,0},{8,2},{10,4},{12,6},{14,8},{16,10},{18,12},{20,14},{22,16},{... | collective-permute-start | bytes 2359304 | tf_op jit(solution)/shard_map/ppermute | solution.py:17
  138.3 1.9 copy-start.9
  138.3 1.9 copy-start.11
  142.3 5.7 copy-start.13
  150.8 1216.5 %all-reduce.5.cloned.1.call-start = ((), (), s32[]{:S(2)}) async-start(), calls=%async_computation.3 | async-start | bytes 9437184 | tf_op jit(solution)/shard_map/psum | solution.py:104
  1367.2 3.2 copy-start.2
  (2 other events, 1.9 us)
Sparse Core Ops, SparseCore 0:
  12.6 45.1 all-gather.2
  101.2 29.0 reduce-scatter.1
  150.9 132.6 all-reduce.6
  286.1 1081.0 all-reduce.4
